TPU v7x, 32 devices: a whole 2x2x4 slice. The times are simulated.
32 devices in a mesh: grp: 2 (over y), gx: 4 (over z), gy: 2 (over x), gz: 2 (over core).
Axes of the slice: x: 2, y: 2, z: 4, core: 2. Of those that a mesh axis runs over, the one named last changes fastest.
Arguments:
- parcel_values: bfloat16 [6, 131072], P(None, ('grp', 'gx', 'gy', 'gz')), parts along dimension 1, may hold values from -2304 to 2304
- parcel_owner: int32 [131072, 1], P(('grp', 'gx', 'gy', 'gz')), parts along dimension 0, may hold values from 0 to 3; in each aligned block of 4096 rows (0 to 4095, 4096 to 8191, ...) at most 1536 rows name the same one
- parcel_cell: int32 [131072], P(('grp', 'gx', 'gy', 'gz')), parts along dimension 0, may hold values from 0 to 65535
- live_counts: int32 [32], P(('grp', 'gx', 'gy', 'gz')), parts along dimension 0, may hold values from 1 to 4096, 49152 in all
- fluid_state: bfloat16 [6, 256, 32, 256], P(None, ('grp', 'gx'), 'gy', 'gz'), parts along dimension 1, may hold values from -6 to 6
Outputs:
- coupled: bfloat16 [6, 256, 32, 256], P(None, ('grp', 'gx'), 'gy', 'gz'), parts along dimension 1
There are 2 independent parts, one for each index of `grp`. A program takes and returns all parts, laid end to end along the dimension named above; each array names one. Nothing has to cross between parts.
Inputs may be any that keep to these rules, and one draw needn't show every extreme that they name: `parcel_owner`: among the rows of one brick no streamwise index is named by more than 1536 rows; some brick names one exactly 1536 times. `parcel_cell`: cells are numbered (x * 16 + y) * 128 + z within the brick. `live_counts`: A brick's live parcels are its first rows; some brick has all rows live.
All inputs are finite; a program needn't handle non-finite values. No bound on the sum of `live_counts` on one device may be relied on, other than what follows from the above.
Results may differ from a plain program's by a relative error of at most 0.005.
Values may be sent and summed in bfloat16 or wider, within the bound.
A program may use at most 64 MiB of HBM per device.

v0:
```python
import jax
import jax.numpy as jnp
from jax import lax
from jax.sharding import PartitionSpec as P

REACH = 16
spread_cells = 12.0


def padded(shard, sides, width):
    for axis, dim in sides:
        size, length = (lax.axis_size(axis), shard.shape[dim])
        up = [(i, (i + 1) % size) for i in range(size)]
        down = [(j, i) for i, j in up]
        last = lax.slice_in_dim(shard, length - width, length, axis=dim)
        initial = lax.slice_in_dim(shard, 0, width, axis=dim)
        before = lax.ppermute(last, axis, up)
        after = lax.ppermute(initial, axis, down)
        shard = jnp.concatenate([before, shard, after], axis=dim)
    return shard


def tap_curve(offsets):
    tap_grid = jnp.arange(2 * REACH + 1).astype(jnp.float32)
    tap_sum = jnp.sum(
        jnp.exp(-(tap_grid - REACH) * (tap_grid - REACH) / (2.0 * spread_cells * spread_cells))
    )
    return (
        jnp.exp(-(offsets - REACH) * (offsets - REACH) / (2.0 * spread_cells * spread_cells))
        / tap_sum
    )


def banded(out_rows, in_rows, shift):
    row_ids = lax.broadcasted_iota(jnp.int32, (out_rows, in_rows), 0)
    col_ids = lax.broadcasted_iota(jnp.int32, (out_rows, in_rows), 1)
    offset_ids = col_ids - row_ids + shift
    inside = (offset_ids >= 0) & (offset_ids <= 2 * REACH)
    values = tap_curve(offset_ids.astype(jnp.float32)).astype(jnp.bfloat16)
    return jnp.where(inside, values, jnp.zeros_like(values))


def on_device(parcel_values, parcel_owner, parcel_cell, live_counts, fluid_state):
    channels, count_dev = parcel_values.shape
    width_x, width_y, width_z = (fluid_state.shape[1], fluid_state.shape[2], fluid_state.shape[3])
    owners = lax.axis_size("gx")
    capacity = 3 * count_dev // (2 * owners)
    owner_ids = parcel_owner[:, 0]
    local_rows = jnp.arange(count_dev, dtype=jnp.int32)
    is_live = local_rows < live_counts[0]
    owner_hits = (
        (owner_ids[:, None] == jnp.arange(owners, dtype=jnp.int32)[None, :]) & is_live[:, None]
    ).astype(jnp.int32)
    position = jnp.sum(jnp.cumsum(owner_hits, axis=0) * owner_hits, axis=1) - 1
    slot_index = jnp.where(is_live, owner_ids * capacity + position, owners * capacity)
    cell_xpart = (parcel_cell // (width_y * width_z)).astype(jnp.bfloat16)
    cell_ypart = (parcel_cell // width_z % width_y).astype(jnp.bfloat16)
    cell_low = (parcel_cell % width_z).astype(jnp.bfloat16)
    send_rows = jnp.concatenate(
        [parcel_values, cell_xpart[None, :], cell_ypart[None, :], cell_low[None, :]], axis=0
    )
    packed = (
        jnp.zeros((channels + 3, owners * capacity), jnp.bfloat16)
        .at[:, slot_index]
        .set(send_rows, mode="drop")
    )
    packed = packed.reshape(channels + 3, owners, capacity)
    arrived = lax.all_to_all(packed, "gx", split_axis=1, concat_axis=1, tiled=True).reshape(
        channels + 3, owners * capacity
    )
    slot_total = owners * capacity
    block_rows = min(1024, slot_total)
    plane_cells = width_x * width_y
    high_grid = jnp.arange(plane_cells, dtype=jnp.float32)
    low_grid = jnp.arange(width_z, dtype=jnp.float32)

    def deposit(step_index, summed):
        window = lax.dynamic_slice_in_dim(arrived, step_index * block_rows, block_rows, 1)
        high_ids = window[channels].astype(jnp.float32) * width_y + window[channels + 1].astype(
            jnp.float32
        )
        high_hot = (high_ids[:, None] == high_grid[None, :]).astype(jnp.bfloat16)
        low_hot = (window[channels + 2].astype(jnp.float32)[:, None] == low_grid[None, :]).astype(
            jnp.bfloat16
        )
        weighted = window[:channels][:, :, None] * low_hot[None, :, :]
        return summed + jnp.einsum(
            "sh,csz->chz", high_hot, weighted, preferred_element_type=jnp.float32
        )

    summed = lax.fori_loop(
        0,
        slot_total // block_rows,
        deposit,
        jnp.zeros((channels, plane_cells, width_z), jnp.float32),
    )
    source = summed.reshape(channels, width_x, width_y, width_z).astype(jnp.bfloat16)
    flat_source = source.reshape(channels, width_x, width_y * width_z)
    pencil = lax.all_to_all(flat_source, "gx", split_axis=2, concat_axis=1, tiled=True)
    full_x = pencil.shape[1]
    smoothed = jnp.einsum(
        "ij,cjk->cik", banded(full_x, full_x, REACH), pencil, preferred_element_type=jnp.float32
    ).astype(jnp.bfloat16)
    after_x = lax.all_to_all(smoothed, "gx", split_axis=1, concat_axis=2, tiled=True)
    after_x = after_x.reshape(channels, width_x, width_y, width_z)
    extended_y = padded(after_x, (("gy", 2),), REACH)
    after_y = jnp.einsum(
        "ij,cxjz->cxiz",
        banded(width_y, width_y + 2 * REACH, 0),
        extended_y,
        preferred_element_type=jnp.float32,
    ).astype(jnp.bfloat16)
    extended_z = padded(after_y, (("gz", 3),), REACH)
    smooth_z = jnp.einsum(
        "cxyj,ij->cxyi",
        extended_z,
        banded(width_z, width_z + 2 * REACH, 0),
        preferred_element_type=jnp.float32,
    )
    return (fluid_state.astype(jnp.float32) + smooth_z).astype(jnp.bfloat16)


def solution(mesh):
    in_specs = (
        P(None, ("grp", "gx", "gy", "gz")),
        P(("grp", "gx", "gy", "gz"), None),
        P(("grp", "gx", "gy", "gz")),
        P(("grp", "gx", "gy", "gz")),
        P(None, ("grp", "gx"), "gy", "gz"),
    )
    out_specs = P(None, ("grp", "gx"), "gy", "gz")
    return jax.shard_map(
        on_device, mesh=mesh, in_specs=in_specs, out_specs=out_specs, check_vma=False
    )
```

profile of v0, /device:TPU:0, one launch (start us, length us, event | category | flops | bytes accessed | tf_op | source)
XLA Modules:
  0.0 157.6 jit_solution(1705467644931148753)
XLA Ops:
  0.7 0.7 fusion.61
  1.4 1.2 reduce-window.6
  2.6 0.2 slice_reduce_fusion
  2.8 0.2 reduce-window.9
  3.1 0.8 fusion.53
  3.9 0.8 fusion.79
  4.8 0.9 maximum_bitcast_fusion
  5.7 0.5 copy.30
  6.3 11.4 %scatter_custom_fusion = bf16[9,6144]{0,1:T(8,128)(2,1)S(1)} fusion(s32[4096]{0:T(1024)S(1)} %bitcast.85, bf16[4096,9]{1,0:T(8,128)(2,1)S(1)} %copy.30, bf16[]{:T(256)} %constant.117.clone.1), kind=kCustom, calls=%fused_computation.36 | custom fusion | bytes 110594 | tf_op jit(solution)/shard_map/scatter | solution.py:65
  17.6 1.4 copy.31
  19.0 6.3 %all-to-all-start = ((bf16[9,4,1536]{2,0,1:T(8,128)(2,1)}), bf16[9,4,1536]{2,0,1:T(8,128)(2,1)S(1)}, u32[]{:S(2)}, u32[]{:S(2)}) async-start(bf16[9,4,1536]{2,0,1:T(8,128)(2,1)} %copy.31), calls=%async_computation | async-start | bytes 393216 | tf_op jit(solution)/shard_map/all_to_all | solution.py:68
  25.3 7.5 %all-to-all-done = bf16[9,4,1536]{2,0,1:T(8,128)(2,1)S(1)} async-done(((bf16[9,4,1536]{2,0,1:T(8,128)(2,1)}), bf16[9,4,1536]{2,0,1:T(8,128)(2,1)S(1)}, u32[]{:S(2)}, u32[]{:S(2)}) %all-to-all-start) | async-done | bytes 110624 | tf_op jit(solution)/shard_map/all_to_all | solution.py:68
  33.1 9.3 %while.14 = (s32[]{:T(128)}, f32[6,512,128]{1,2,0:T(8,128)S(1)}, bf16[9,6144]{1,0:T(8,128)(2,1)S(1)}, s32[]{:T(128)}, s32[]{:T(128)}, /*index=5*/s32[]{}, s32[]{:T(128)}, s32[]{:T(128)}, s32[]{}, s32[]{}) while((s32[]{:T(128)}, f32[6,512,128]{1,2,0:T(8,128)S(1)}, bf16[9,6144]{1,0:T(8,128)(2,1)S(1)}, s32[]{:T(128)}, s32[]{:T(128)}, ...), condition=%wide.region_5.6_spmd.clone, body=%wide.region_4.5_spmd.clone.sunk | while | flops 807670784 | bytes 3729625 | solution.py:91
  33.3 1.3 bitcast_add_fusion.2
  34.8 1.3 bitcast_add_fusion.2
  36.4 1.3 bitcast_add_fusion.2
  37.9 1.3 bitcast_add_fusion.2
  39.5 1.3 bitcast_add_fusion.2
  41.0 1.3 bitcast_add_fusion.2
  42.5 0.4 copy.33
  42.8 0.3 convert_element_type.120
  43.2 4.2 %copy.34 = bf16[6,32,2048]{1,0,2:T(8,128)(2,1)} copy(bf16[6,32,2048]{2,1,0:T(8,128)(2,1)S(1)} %convert_element_type.120) | data formatting | bytes 1572864 | tf_op jit(solution)/shard_map/convert_element_type | solution.py:97
  47.4 5.7 %reshape.138 = bf16[4,2,49152]{2,1,0:T(2,128)(2,1)} reshape(bf16[2048,6,32]{2,1,0:T(8,128)(2,1)} %bitcast.72) | data formatting | bytes 1572864
  53.1 3.5 %all-to-all-start.1 = ((bf16[4,2,49152]{2,1,0:T(2,128)(2,1)}), bf16[4,2,49152]{2,1,0:T(2,128)(2,1)S(1)}, u32[]{:S(2)}, u32[]{:S(2)}) async-start(bf16[4,2,49152]{2,1,0:T(2,128)(2,1)} %reshape.138), calls=%async_computation.1 | async-start | bytes 1572864 | tf_op jit(solution)/shard_map/all_to_all | solution.py:99
  56.6 0.6 fusion.104
  57.2 18.1 %all-to-all-done.1 = bf16[4,2,49152]{2,1,0:T(2,128)(2,1)S(1)} async-done(((bf16[4,2,49152]{2,1,0:T(2,128)(2,1)}), bf16[4,2,49152]{2,1,0:T(2,128)(2,1)S(1)}, u32[]{:S(2)}, u32[]{:S(2)}) %all-to-all-start.1) | async-done | bytes 786464 | tf_op jit(solution)/shard_map/all_to_all | solution.py:99
  75.3 4.2 %reshape.139 = bf16[2048,6,32]{2,1,0:T(8,128)(2,1)} reshape(bf16[4,2,49152]{2,1,0:T(2,128)(2,1)S(1)} %all-to-all-done.1) | data formatting | bytes 1572864
  79.5 4.5 %copy.48 = bf16[6,32,4,512]{3,2,1,0:T(4,128)(2,1)S(1)} copy(bf16[6,32,4,512]{1,0,3,2:T(8,128)(2,1)} %bitcast.73) | data formatting | bytes 1572864 | tf_op jit(solution)/shard_map/all_to_all | solution.py:99
  84.0 0.2 copy.36
  84.2 1.0 fusion.38
  85.2 0.9 copy.38
  86.1 27.7 %all_to_all.38 = bf16[6,128,512]{2,0,1:T(8,128)(2,1)S(1)} all-to-all(bf16[6,128,512]{2,0,1:T(8,128)(2,1)S(1)} %copy.38), channel_id=1, replica_groups=mesh['grp'=2,'gx'=4,'gy'=2,'gz'=2] {'gx'}, dimensions={1} | all-to-all | bytes 1572864 | tf_op jit(solution)/shard_map/all_to_all | solution.py:104
  113.8 0.6 copy.40
  114.4 0.3 reshape.120
  114.7 1.6 collective-permute-start
  116.2 0.5 collective-permute-start.1
  116.8 18.5 %collective-permute-done = bf16[6,32,16,128]{3,2,1,0:T(8,128)(2,1)S(1)} collective-permute-done((bf16[6,32,16,128]{3,2,1,0:T(8,128)(2,1)S(1)}, bf16[6,32,16,128]{3,2,1,0:T(8,128)(2,1)S(1)}, u32[]{:S(2)}, u32[]{:S(2)}) %collective-permute-start) | collective-permute-done | bytes 786464 | tf_op jit(solution)/shard_map/ppermute | solution.py:17
  135.2 14.4 %collective-permute-done.1 = bf16[6,32,16,128]{3,2,1,0:T(8,128)(2,1)S(1)} collective-permute-done((bf16[6,32,16,128]{3,2,1,0:T(8,128)(2,1)S(1)}, bf16[6,32,16,128]{3,2,1,0:T(8,128)(2,1)S(1)}, u32[]{:S(2)}, u32[]{:S(2)}) %collective-permute-start.1) | collective-permute-done | bytes 786464 | tf_op jit(solution)/shard_map/ppermute | solution.py:18
  149.7 1.1 fusion.35
  150.7 0.4 fusion.123
  151.1 0.6 copy.41
  151.8 0.6 copy.42
  152.5 0.5 collective-permute-start.3
  153.0 0.5 collective-permute-done.2
  153.5 0.6 copy.43
  154.2 0.2 collective-permute-done.3
  154.3 0.6 copy.44
  155.0 2.6 %add_convert_fusion = bf16[6,32,16,128]{3,2,1,0:T(8,128)(2,1)} fusion(bf16[6,32,16,128]{3,2,1,0:T(8,128)(2,1)S(1)} %copy-done.1, bf16[6,32,16,16]{3,2,1,0:T(8,128)(2,1)S(1)} %copy.44, bf16[6,32,16,128]{3,2,1,0:T(8,128)(2,1)S(1)} %fusion.35, bf16[6,32,16,16]{3,2,1,0:T(8,128)(2,1)S(1)} %copy.43, f32[]{:T(128)} %fusion.104), kind=kOutput, calls=%fused_computation.31 | convolution fusion | flops 130203648 | bytes 2555908 | tf_op jit(solution)/shard_map/cxyj,ij->cxyi/dot_general | solution.py:114
  (42 shorter events, 1.6 us)
Async XLA Ops:
  0.0 6.2 %copy-start = (s32[4096,1]{0,1:T(1,128)S(1)}, s32[4096,1]{0,1:T(1,128)}, u32[]{:S(2)}) copy-start(s32[4096,1]{0,1:T(1,128)} %param.8) | copy-start | bytes 49156
  19.0 13.8 %all-to-all-start = ((bf16[9,4,1536]{2,0,1:T(8,128)(2,1)}), bf16[9,4,1536]{2,0,1:T(8,128)(2,1)S(1)}, u32[]{:S(2)}, u32[]{:S(2)}) async-start(bf16[9,4,1536]{2,0,1:T(8,128)(2,1)} %copy.31), calls=%async_computation | async-start | bytes 393216 | tf_op jit(solution)/shard_map/all_to_all | solution.py:68
  53.1 22.2 %all-to-all-start.1 = ((bf16[4,2,49152]{2,1,0:T(2,128)(2,1)}), bf16[4,2,49152]{2,1,0:T(2,128)(2,1)S(1)}, u32[]{:S(2)}, u32[]{:S(2)}) async-start(bf16[4,2,49152]{2,1,0:T(2,128)(2,1)} %reshape.138), calls=%async_computation.1 | async-start | bytes 1572864 | tf_op jit(solution)/shard_map/all_to_all | solution.py:99
  114.7 20.5 %collective-permute-start = (bf16[6,32,16,128]{3,2,1,0:T(8,128)(2,1)S(1)}, bf16[6,32,16,128]{3,2,1,0:T(8,128)(2,1)S(1)}, u32[]{:S(2)}, u32[]{:S(2)}) collective-permute-start(bf16[6,32,16,128]{3,2,1,0:T(8,128)(2,1)S(1)} %reshape.120), channel_id=1, source_target_pairs={{0,2},{2,0},{1,3},{3,1},{4,6},{6,4},{5,7},{7,5},{8,10},{10,8},{9,1... | collective-permute-start | bytes 2359304 | tf_op jit(solution)/shard_map/ppermute | solution.py:17
  116.2 33.4 %collective-permute-start.1 = (bf16[6,32,16,128]{3,2,1,0:T(8,128)(2,1)S(1)}, bf16[6,32,16,128]{3,2,1,0:T(8,128)(2,1)S(1)}, u32[]{:S(2)}, u32[]{:S(2)}) collective-permute-start(bf16[6,32,16,128]{3,2,1,0:T(8,128)(2,1)S(1)} %reshape.120), channel_id=1, source_target_pairs={{2,0},{0,2},{3,1},{1,3},{6,4},{4,6},{7,5},{5,7},{10,8},{8,10},{11,... | collective-permute-start | bytes 2359304 | tf_op jit(solution)/shard_map/ppermute | solution.py:18
  151.7 1.8 %collective-permute-start.2 = (bf16[6,32,16,16]{1,3,2,0:T(8,128)(2,1)S(1)}, bf16[6,32,16,16]{1,3,2,0:T(8,128)(2,1)S(1)}, u32[]{:S(2)}, u32[]{:S(2)}) collective-permute-start(bf16[6,32,16,16]{1,3,2,0:T(8,128)(2,1)S(1)} %copy.41), channel_id=1, source_target_pairs={{0,1},{1,0},{2,3},{3,2},{4,5},{5,4},{6,7},{7,6},{8,9},{9,8},{10,11... | collective-permute-start | bytes 294920 | tf_op jit(solution)/shard_map/ppermute | solution.py:17
  151.8 3.2 %copy-start.1 = (bf16[6,32,16,128]{3,2,1,0:T(8,128)(2,1)S(1)}, bf16[6,32,16,128]{3,2,1,0:T(8,128)(2,1)}, u32[]{:S(2)}) copy-start(bf16[6,32,16,128]{3,2,1,0:T(8,128)(2,1)} %param.11) | copy-start | bytes 2359300
  152.5 1.9 %collective-permute-start.3 = (bf16[6,32,16,16]{1,3,2,0:T(8,128)(2,1)S(1)}, bf16[6,32,16,16]{1,3,2,0:T(8,128)(2,1)S(1)}, u32[]{:S(2)}, u32[]{:S(2)}) collective-permute-start(bf16[6,32,16,16]{1,3,2,0:T(8,128)(2,1)S(1)} %copy.42), channel_id=1, source_target_pairs={{1,0},{0,1},{3,2},{2,3},{5,4},{4,5},{7,6},{6,7},{9,8},{8,9},{11,10... | collective-permute-start | bytes 294920 | tf_op jit(solution)/shard_map/ppermute | solution.py:18
where the time goes:
time: 158 us
  waiting for transfers between devices  59.2 us (37%)
  local copies, waits for them, and re-layouts  37.9 us (24%)
  blocking collectives  27.7 us (18%)
  matrix products  12.6 us (8%)
  starting transfers between devices  12.5 us (8%)
  other arithmetic  6.49 us (4%)
    all_to_all x1, blocking collectives, on_device(): lax.all_to_all(smoothed, 'gx', split_axis=1, concat_axis=2, tiled=True)  27.7 us
    ppermute x2, waiting for transfers between devices, padded(): before = lax.ppermute(last, axis, up)  19 us
    all_to_all x1, waiting for transfers between devices, on_device(): lax.all_to_all(flat_source, 'gx', split_axis=2, concat_axis=1, tiled=True)  18.1 us
    ppermute x2, waiting for transfers between devices, padded(): after = lax.ppermute(initial, axis, down)  14.6 us
    scatter x1, local copies, waits for them, and re-layouts, on_device(): packed = jnp.zeros((channels + 3, owners * capacity), jnp.bfloat16).at[:,...  11.4 us
    unnamed x8, local copies, waits for them, and re-layouts  9.98 us
    dot_general x6, matrix products, deposit(): jnp.einsum('sh,csz->chz', high_hot, weighted, preferred_element_type=jnp....  7.91 us
    all_to_all x1, waiting for transfers between devices, on_device(): lax.all_to_all(packed, 'gx', split_axis=1, concat_axis=1, tiled=True)  7.51 us
  transfers between devices with their start and end apart: 6, of which 6 were waited for; matrix products, arithmetic and copies ran while one was open for 1% of the time, Pallas kernels for 0%

commit v1 on v0

--- a/solution.py
+++ b/solution.py
@@ -101,7 +101,10 @@
     smoothed = jnp.einsum(
         "ij,cjk->cik", banded(full_x, full_x, REACH), pencil, preferred_element_type=jnp.float32
     ).astype(jnp.bfloat16)
-    after_x = lax.all_to_all(smoothed, "gx", split_axis=1, concat_axis=2, tiled=True)
+    after_x = jnp.concatenate(
+        lax.all_to_all(jnp.stack(jnp.split(smoothed, lax.axis_size("gx"), axis=1)), "gx", 0, 0),
+        axis=2,
+    )
     after_x = after_x.reshape(channels, width_x, width_y, width_z)
     extended_y = padded(after_x, (("gy", 2),), REACH)
     after_y = jnp.einsum(

time: 158 us -> 152 us (0.962)
  blocking collectives: 27.7 us -> 22.1 us
    all_to_all x1, blocking collectives: 27.7 us -> 22.1 us  [on_device(): lax.all_to_all(jnp.stack(jnp.split(smoothed, lax.axis_size('gx'), axis=1)...]
where the time goes in v1:
time: 152 us; the launch traced here: 151 us
  waiting for transfers between devices  59.2 us (39%)
  local copies, waits for them, and re-layouts  37.1 us (24%)
  blocking collectives  22.1 us (15%)
  matrix products  12.6 us (8%)
  starting transfers between devices  12.5 us (8%)
  other arithmetic  6.6 us (4%)
    all_to_all x1, blocking collectives, on_device(): lax.all_to_all(jnp.stack(jnp.split(smoothed, lax.axis_size('gx'), axis=1)...  22.1 us
    ppermute x2, waiting for transfers between devices, padded(): before = lax.ppermute(last, axis, up)  19 us
    all_to_all x1, waiting for transfers between devices, on_device(): lax.all_to_all(flat_source, 'gx', split_axis=2, concat_axis=1, tiled=True)  18.1 us
    ppermute x2, waiting for transfers between devices, padded(): after = lax.ppermute(initial, axis, down)  14.6 us
    scatter x1, local copies, waits for them, and re-layouts, on_device(): packed = jnp.zeros((channels + 3, owners * capacity), jnp.bfloat16).at[:,...  11.4 us
    unnamed x8, local copies, waits for them, and re-layouts  9.98 us
    dot_general x6, matrix products, deposit(): jnp.einsum('sh,csz->chz', high_hot, weighted, preferred_element_type=jnp....  7.91 us
    all_to_all x1, waiting for transfers between devices, on_device(): lax.all_to_all(packed, 'gx', split_axis=1, concat_axis=1, tiled=True)  7.51 us
  transfers between devices with their start and end apart: 6, of which 6 were waited for; matrix products, arithmetic and copies ran while one was open for 1% of the time, Pallas kernels for 0%

profile of v1, /device:TPU:0, one launch (start us, length us, event | category | flops | bytes accessed | tf_op | source)
XLA Modules:
  0.0 151.2 jit_solution(13293237900098828716)
XLA Ops:
  0.7 0.7 fusion.61
  1.4 1.2 reduce-window.6
  2.6 0.2 slice_reduce_fusion
  2.8 0.2 reduce-window.9
  3.1 0.8 fusion.53
  3.9 0.8 fusion.79
  4.8 0.9 maximum_bitcast_fusion
  5.7 0.5 copy.24
  6.3 11.4 %scatter_custom_fusion = bf16[9,6144]{0,1:T(8,128)(2,1)S(1)} fusion(s32[4096]{0:T(1024)S(1)} %bitcast.91, bf16[4096,9]{1,0:T(8,128)(2,1)S(1)} %copy.24, bf16[]{:T(256)} %constant.117.clone.1), kind=kCustom, calls=%fused_computation.37 | custom fusion | bytes 110594 | tf_op jit(solution)/shard_map/scatter | solution.py:65
  17.6 1.4 copy.25
  19.0 6.3 %all-to-all-start = ((bf16[9,4,1536]{2,0,1:T(8,128)(2,1)}), bf16[9,4,1536]{2,0,1:T(8,128)(2,1)S(1)}, u32[]{:S(2)}, u32[]{:S(2)}) async-start(bf16[9,4,1536]{2,0,1:T(8,128)(2,1)} %copy.25), calls=%async_computation | async-start | bytes 393216 | tf_op jit(solution)/shard_map/all_to_all | solution.py:68
  25.3 7.5 %all-to-all-done = bf16[9,4,1536]{2,0,1:T(8,128)(2,1)S(1)} async-done(((bf16[9,4,1536]{2,0,1:T(8,128)(2,1)}), bf16[9,4,1536]{2,0,1:T(8,128)(2,1)S(1)}, u32[]{:S(2)}, u32[]{:S(2)}) %all-to-all-start) | async-done | bytes 110624 | tf_op jit(solution)/shard_map/all_to_all | solution.py:68
  33.1 9.3 %while.14 = (s32[]{:T(128)}, f32[6,512,128]{1,2,0:T(8,128)S(1)}, bf16[9,6144]{1,0:T(8,128)(2,1)S(1)}, s32[]{:T(128)}, s32[]{:T(128)}, /*index=5*/s32[]{}, s32[]{:T(128)}, s32[]{:T(128)}, s32[]{}, s32[]{}) while((s32[]{:T(128)}, f32[6,512,128]{1,2,0:T(8,128)S(1)}, bf16[9,6144]{1,0:T(8,128)(2,1)S(1)}, s32[]{:T(128)}, s32[]{:T(128)}, ...), condition=%wide.region_5.6_spmd.clone, body=%wide.region_4.5_spmd.clone.sunk | while | flops 807670784 | bytes 3729625 | solution.py:91
  33.3 1.3 bitcast_add_fusion.2
  34.8 1.3 bitcast_add_fusion.2
  36.4 1.3 bitcast_add_fusion.2
  37.9 1.3 bitcast_add_fusion.2
  39.5 1.3 bitcast_add_fusion.2
  41.0 1.3 bitcast_add_fusion.2
  42.5 0.4 copy.27
  42.8 0.3 convert_element_type.120
  43.2 4.2 %copy.28 = bf16[6,32,2048]{1,0,2:T(8,128)(2,1)} copy(bf16[6,32,2048]{2,1,0:T(8,128)(2,1)S(1)} %convert_element_type.120) | data formatting | bytes 1572864 | tf_op jit(solution)/shard_map/convert_element_type | solution.py:97
  47.4 5.7 %reshape.137 = bf16[4,2,49152]{2,1,0:T(2,128)(2,1)} reshape(bf16[2048,6,32]{2,1,0:T(8,128)(2,1)} %bitcast.78) | data formatting | bytes 1572864
  53.1 3.5 %all-to-all-start.1 = ((bf16[4,2,49152]{2,1,0:T(2,128)(2,1)}), bf16[4,2,49152]{2,1,0:T(2,128)(2,1)S(1)}, u32[]{:S(2)}, u32[]{:S(2)}) async-start(bf16[4,2,49152]{2,1,0:T(2,128)(2,1)} %reshape.137), calls=%async_computation.1 | async-start | bytes 1572864 | tf_op jit(solution)/shard_map/all_to_all | solution.py:99
  56.6 0.6 fusion.104
  57.2 18.1 %all-to-all-done.1 = bf16[4,2,49152]{2,1,0:T(2,128)(2,1)S(1)} async-done(((bf16[4,2,49152]{2,1,0:T(2,128)(2,1)}), bf16[4,2,49152]{2,1,0:T(2,128)(2,1)S(1)}, u32[]{:S(2)}, u32[]{:S(2)}) %all-to-all-start.1) | async-done | bytes 786464 | tf_op jit(solution)/shard_map/all_to_all | solution.py:99
  75.3 4.2 %reshape.138 = bf16[2048,6,32]{2,1,0:T(8,128)(2,1)} reshape(bf16[4,2,49152]{2,1,0:T(2,128)(2,1)S(1)} %all-to-all-done.1) | data formatting | bytes 1572864
  79.5 4.5 %copy.38 = bf16[6,32,4,512]{3,2,1,0:T(4,128)(2,1)S(1)} copy(bf16[6,32,4,512]{1,0,3,2:T(8,128)(2,1)} %bitcast.79) | data formatting | bytes 1572864 | tf_op jit(solution)/shard_map/all_to_all | solution.py:99
  84.0 0.2 copy.30
  84.2 1.0 fusion.38
  85.2 0.1 pad_maximum_fusion
  85.3 22.1 %all_to_all.28 = bf16[4,6,32,512]{3,2,1,0:T(8,128)(2,1)S(1)} all-to-all(bf16[4,6,32,512]{3,2,1,0:T(8,128)(2,1)S(1)} %pad_maximum_fusion), channel_id=1, replica_groups=mesh['grp'=2,'gx'=4,'gy'=2,'gz'=2] {'gx'}, dimensions={0} | all-to-all | bytes 1572864 | tf_op jit(solution)/shard_map/all_to_all | solution.py:105
  107.4 0.6 copy.31
  108.0 0.3 reshape_reshape.3
  108.3 1.6 %collective-permute-start = (bf16[6,32,16,128]{3,2,1,0:T(8,128)(2,1)S(1)}, bf16[6,32,16,128]{3,2,1,0:T(8,128)(2,1)S(1)}, u32[]{:S(2)}, u32[]{:S(2)}) collective-permute-start(bf16[6,32,16,128]{3,2,1,0:T(8,128)(2,1)S(1)} %reshape_reshape.3), channel_id=1, source_target_pairs={{0,2},{2,0},{1,3},{3,1},{4,6},{6,4},{5,7},{7,5},{8,10},{10,8},{9,1... | collective-permute-start | bytes 2359304 | tf_op jit(solution)/shard_map/ppermute | solution.py:17
  109.9 0.5 collective-permute-start.1
  110.4 18.5 %collective-permute-done = bf16[6,32,16,128]{3,2,1,0:T(8,128)(2,1)S(1)} collective-permute-done((bf16[6,32,16,128]{3,2,1,0:T(8,128)(2,1)S(1)}, bf16[6,32,16,128]{3,2,1,0:T(8,128)(2,1)S(1)}, u32[]{:S(2)}, u32[]{:S(2)}) %collective-permute-start) | collective-permute-done | bytes 786464 | tf_op jit(solution)/shard_map/ppermute | solution.py:17
  128.8 14.4 %collective-permute-done.1 = bf16[6,32,16,128]{3,2,1,0:T(8,128)(2,1)S(1)} collective-permute-done((bf16[6,32,16,128]{3,2,1,0:T(8,128)(2,1)S(1)}, bf16[6,32,16,128]{3,2,1,0:T(8,128)(2,1)S(1)}, u32[]{:S(2)}, u32[]{:S(2)}) %collective-permute-start.1) | collective-permute-done | bytes 786464 | tf_op jit(solution)/shard_map/ppermute | solution.py:18
  143.3 1.1 fusion.35
  144.4 0.4 fusion.123
  144.7 0.6 copy.32
  145.5 0.6 copy.33
  146.1 0.5 collective-permute-start.3
  146.6 0.5 collective-permute-done.2
  147.1 0.6 copy.34
  147.8 0.2 collective-permute-done.3
  148.0 0.6 copy.35
  148.6 2.6 %add_convert_fusion = bf16[6,32,16,128]{3,2,1,0:T(8,128)(2,1)} fusion(bf16[6,32,16,128]{3,2,1,0:T(8,128)(2,1)S(1)} %copy-done.1, bf16[6,32,16,16]{3,2,1,0:T(8,128)(2,1)S(1)} %copy.35, bf16[6,32,16,128]{3,2,1,0:T(8,128)(2,1)S(1)} %fusion.35, bf16[6,32,16,16]{3,2,1,0:T(8,128)(2,1)S(1)} %copy.34, f32[]{:T(128)} %fusion.104), kind=kOutput, calls=%fused_computation.31 | convolution fusion | flops 130203648 | bytes 2555908 | tf_op jit(solution)/shard_map/cxyj,ij->cxyi/dot_general | solution.py:117
  (43 shorter events, 1.7 us)
Async XLA Ops:
  0.0 6.2 %copy-start = (s32[4096,1]{0,1:T(1,128)S(1)}, s32[4096,1]{0,1:T(1,128)}, u32[]{:S(2)}) copy-start(s32[4096,1]{0,1:T(1,128)} %param.8) | copy-start | bytes 49156
  19.0 13.8 %all-to-all-start = ((bf16[9,4,1536]{2,0,1:T(8,128)(2,1)}), bf16[9,4,1536]{2,0,1:T(8,128)(2,1)S(1)}, u32[]{:S(2)}, u32[]{:S(2)}) async-start(bf16[9,4,1536]{2,0,1:T(8,128)(2,1)} %copy.25), calls=%async_computation | async-start | bytes 393216 | tf_op jit(solution)/shard_map/all_to_all | solution.py:68
  53.1 22.2 %all-to-all-start.1 = ((bf16[4,2,49152]{2,1,0:T(2,128)(2,1)}), bf16[4,2,49152]{2,1,0:T(2,128)(2,1)S(1)}, u32[]{:S(2)}, u32[]{:S(2)}) async-start(bf16[4,2,49152]{2,1,0:T(2,128)(2,1)} %reshape.137), calls=%async_computation.1 | async-start | bytes 1572864 | tf_op jit(solution)/shard_map/all_to_all | solution.py:99
  108.3 20.5 %collective-permute-start = (bf16[6,32,16,128]{3,2,1,0:T(8,128)(2,1)S(1)}, bf16[6,32,16,128]{3,2,1,0:T(8,128)(2,1)S(1)}, u32[]{:S(2)}, u32[]{:S(2)}) collective-permute-start(bf16[6,32,16,128]{3,2,1,0:T(8,128)(2,1)S(1)} %reshape_reshape.3), channel_id=1, source_target_pairs={{0,2},{2,0},{1,3},{3,1},{4,6},{6,4},{5,7},{7,5},{8,10},{10,8},{9,1... | collective-permute-start | bytes 2359304 | tf_op jit(solution)/shard_map/ppermute | solution.py:17
  109.9 33.4 %collective-permute-start.1 = (bf16[6,32,16,128]{3,2,1,0:T(8,128)(2,1)S(1)}, bf16[6,32,16,128]{3,2,1,0:T(8,128)(2,1)S(1)}, u32[]{:S(2)}, u32[]{:S(2)}) collective-permute-start(bf16[6,32,16,128]{3,2,1,0:T(8,128)(2,1)S(1)} %reshape_reshape.3), channel_id=1, source_target_pairs={{2,0},{0,2},{3,1},{1,3},{6,4},{4,6},{7,5},{5,7},{10,8},{8,10},{11,... | collective-permute-start | bytes 2359304 | tf_op jit(solution)/shard_map/ppermute | solution.py:18
  145.4 1.8 %collective-permute-start.2 = (bf16[6,32,16,16]{1,3,2,0:T(8,128)(2,1)S(1)}, bf16[6,32,16,16]{1,3,2,0:T(8,128)(2,1)S(1)}, u32[]{:S(2)}, u32[]{:S(2)}) collective-permute-start(bf16[6,32,16,16]{1,3,2,0:T(8,128)(2,1)S(1)} %copy.32), channel_id=1, source_target_pairs={{0,1},{1,0},{2,3},{3,2},{4,5},{5,4},{6,7},{7,6},{8,9},{9,8},{10,11... | collective-permute-start | bytes 294920 | tf_op jit(solution)/shard_map/ppermute | solution.py:17
  145.4 3.2 %copy-start.1 = (bf16[6,32,16,128]{3,2,1,0:T(8,128)(2,1)S(1)}, bf16[6,32,16,128]{3,2,1,0:T(8,128)(2,1)}, u32[]{:S(2)}) copy-start(bf16[6,32,16,128]{3,2,1,0:T(8,128)(2,1)} %param.11) | copy-start | bytes 2359300
  146.1 1.9 %collective-permute-start.3 = (bf16[6,32,16,16]{1,3,2,0:T(8,128)(2,1)S(1)}, bf16[6,32,16,16]{1,3,2,0:T(8,128)(2,1)S(1)}, u32[]{:S(2)}, u32[]{:S(2)}) collective-permute-start(bf16[6,32,16,16]{1,3,2,0:T(8,128)(2,1)S(1)} %copy.33), channel_id=1, source_target_pairs={{1,0},{0,1},{3,2},{2,3},{5,4},{4,5},{7,6},{6,7},{9,8},{8,9},{11,10... | collective-permute-start | bytes 294920 | tf_op jit(solution)/shard_map/ppermute | solution.py:18
